TPU v7x, 128 devices: a whole 4x4x4 slice. The times are simulated.
128 devices in a mesh: group: 16 (over z, y), member: 8 (over x, core).
Axes of the slice: x: 4, y: 4, z: 4, core: 2. Of those that a mesh axis runs over, the one named last changes fastest.
Arguments:
- tokens: bfloat16 [16384, 2048], P(('group', 'member')), may hold values from -6 to 6
- out_grad: bfloat16 [16384, 2048], P(('group', 'member')), may hold values from -6 to 6
- expert_ids: int32 [16384, 10], P(('group', 'member')), may hold values from 0 to 255, all different within a row; in each aligned block of 128 rows (0 to 127, 128 to 255, ...) at most 6 rows name the same one
- gate_vals: float32 [16384, 10], P(('group', 'member')), may hold values from 0.05 to 0.6
- w_gate: bfloat16 [256, 2048, 512], P(('group', 'member')), may hold values from -0.125 to 0.125
- w_up: bfloat16 [256, 2048, 512], P(('group', 'member')), may hold values from -0.125 to 0.125
- w_down: bfloat16 [256, 512, 2048], P(('group', 'member')), may hold values from -0.25 to 0.25
Outputs:
- grad_tokens: bfloat16 [16384, 2048], P(('group', 'member'))
- grad_w_gate: bfloat16 [256, 2048, 512], P(('group', 'member'))
- grad_w_up: bfloat16 [256, 2048, 512], P(('group', 'member'))
- grad_w_down: bfloat16 [256, 512, 2048], P(('group', 'member'))
Inputs may be any that keep to these rules, and one draw needn't show every extreme that they name: `expert_ids`: each row names 10 different experts. Among the rows of one device no expert is named more than 6 times, a bound that some block reaches.
All inputs are finite; a program needn't handle non-finite values.
Results may differ from a plain program's by a relative error of at most 0.019.
Values may be sent and summed in bfloat16 or wider, within the bound.
A program may use at most 192 MiB of HBM per device.

v0:
```python
import jax
import jax.numpy as jnp
from jax import lax
from jax.experimental import pallas as pl
from jax.experimental.pallas import tpu as pltpu
from jax.sharding import PartitionSpec as P

MESH = pl.DeviceIdType.MESH
BF = jnp.bfloat16
F32 = jnp.float32
PARTS = ((0, 768), (768, 640), (1408, 640))
AXES = ((0, 1, 2), (1, 2, 0), (2, 0, 1))
TOK = 128
CAP = 6
ROWS = 8 * CAP
HID = 512
TOPK = 10


def dot(a, b, contract):
    return lax.dot_general(a, b, ((contract[0], contract[1]), ((), ())), preferred_element_type=F32)


NN = ((1,), (0,))
NT = ((1,), (1,))
TN = ((0,), (0,))


def kernel(info, tok, dy, perm_in, wg, wu, wd, out_t, out_g, out_u, out_d, *rest):
    hold_dy, relay = rest[0:3], (rest[3:6], rest[6:9], rest[9:12])
    rest = rest[12:]
    near, send, got = rest[0:3], rest[3:6], (rest[6:9], rest[9:12])
    back, from_sib, last = rest[12:15], rest[15:18], rest[18:21]
    (ids, key, gate, pick, perm, tmp, act, pre, turned, wbuf, loc, ids_s, ids_r, ag_s, ag_r, d_s, d_r, b_s, b_r, z_s,
     z_r, w_sem, o_sem) = rest[21:]

    g = lax.axis_index("group")
    m = lax.axis_index("member")
    zyx = (g // 4, lax.rem(g, 4), m // 2)
    core = lax.rem(m, 2)

    def peer(axis, shift):
        pos = list(zyx)
        pos[axis] = lax.rem(pos[axis] + (shift + 4), 4)
        return (pos[0] * 4 + pos[1], pos[2] * 2 + core)

    sib = (g, zyx[2] * 2 + (1 - core))

    def remote(src, dst, ssem, rsem, to):
        return pltpu.make_async_remote_copy(
            src_ref=src, dst_ref=dst, send_sem=ssem, recv_sem=rsem, device_id=to, device_id_type=MESH
        )

    source = (tok, dy)
    gathered = (near, hold_dy)

    def cols(i):
        return pl.ds(PARTS[i][0], PARTS[i][1])

    def ids_line(i, u):
        return remote(info, ids.at[i, u, core], ids_s.at[i, u], ids_r.at[i, u], peer(AXES[i][0], u))

    def ids_own(i):
        return remote(info, ids.at[i, 0, core], ids_s.at[i, 0], ids_r.at[i, 0], sib)

    def ids_pass(i):
        part = ids.at[i, pl.ds(1, 3), core]
        return remote(part, part, ids_s.at[i, 4], ids_r.at[i, 4], sib)

    def ag_line(t, i, u):
        return remote(source[t].at[:, cols(i)], gathered[t][i].at[u, core], ag_s.at[t, i, u], ag_r.at[t, i, u],
                      peer(AXES[i][0], u))

    def ag_own(t, i):
        return remote(source[t].at[:, cols(i)], gathered[t][i].at[0, core], ag_s.at[t, i, 0], ag_r.at[t, i, 0], sib)

    def ag_pass(t, i, u):
        part = gathered[t][i].at[u, core]
        return remote(part, part, ag_s.at[t, i, 3 + u], ag_r.at[t, i, 3 + u], sib)

    def ag_self(t, i):
        return pltpu.make_async_copy(source[t].at[:, cols(i)], gathered[t][i].at[0, core], loc.at[t, i])

    def refill(i):
        return pltpu.make_async_copy(hold_dy[i], near[i], loc.at[2, i])

    def b0(t, i, e, r):
        k = r - 1
        return remote(send[i].at[e, r, 0], got[t][i].at[e, 0, r], d_s.at[t, i, e, k], d_r.at[t, i, e, k], peer(AXES[i][1], r))

    def b1(t, i, e, r):
        k = r + 2
        return remote(send[i].at[e, r, pl.ds(1, 3)], relay[t][i].at[e, :, r - 1], d_s.at[t, i, e, k], d_r.at[t, i, e, k],
                      peer(AXES[i][1], r))

    def c0(t, i, e, q):
        k = q + 5
        return remote(send[i].at[e, 0, q], got[t][i].at[e, q, 0], d_s.at[t, i, e, k], d_r.at[t, i, e, k], peer(AXES[i][2], q))

    def c1(t, i, e, q):
        k = q + 8
        return remote(relay[t][i].at[e, q - 1], got[t][i].at[e, q, pl.ds(1, 3)], d_s.at[t, i, e, k], d_r.at[t, i, e, k],
                      peer(AXES[i][2], q))

    def rc0(i, e, q):
        k = q - 1
        return remote(send[i].at[e, q, 0], back[i].at[e, 0, q], b_s.at[i, e, k], b_r.at[i, e, k], peer(AXES[i][2], -q))

    def rc1(i, e, q):
        k = q + 2
        return remote(send[i].at[e, q, pl.ds(1, 3)], relay[2][i].at[e, q - 1], b_s.at[i, e, k], b_r.at[i, e, k],
                      peer(AXES[i][2], -q))

    def rb0(i, e, r):
        k = r + 5
        return remote(send[i].at[e, 0, r], back[i].at[e, r, 0], b_s.at[i, e, k], b_r.at[i, e, k], peer(AXES[i][1], -r))

    def rb1(i, e, r):
        k = r + 8
        return remote(relay[2][i].at[e, :, r - 1], back[i].at[e, r, pl.ds(1, 3)], b_s.at[i, e, k], b_r.at[i, e, k],
                      peer(AXES[i][1], -r))

    def z_sib(i):
        return remote(near[i].at[:, 1 - core], from_sib[i], z_s.at[i, 0], z_r.at[i, 0], sib)

    def z_line(i, u):
        return remote(near[i].at[u, core], last[i].at[u - 1], z_s.at[i, u], z_r.at[i, u], peer(AXES[i][0], -u))

    weights = (wg, wu, wd)

    def load_w(n, e):
        return pltpu.make_async_copy(weights[n].at[e], wbuf[n], w_sem.at[n])

    outs = (out_g, out_u, out_d)

    def store_w(n, e):
        return pltpu.make_async_copy(wbuf[n], outs[n].at[e], o_sem.at[n])

    step = (1, 2, 3)

    barrier = pltpu.get_barrier_semaphore()
    for axis in range(3):
        for u in step:
            pl.semaphore_signal(barrier, inc=1, device_id=peer(axis, u), device_id_type=MESH)
    pl.semaphore_signal(barrier, inc=1, device_id=sib, device_id_type=MESH)
    for n in range(3):
        load_w(n, 0).start()
    load_p = pltpu.make_async_copy(perm_in, perm, loc.at[2, 3])
    load_p.start()
    for i in range(3):
        ag_self(0, i).start()
        ag_self(1, i).start()
        ids[i, 0, core] = info[...]
    pl.semaphore_wait(barrier, 10)

    for i in range(3):
        ids_own(i).start()
        for u in step:
            ids_line(i, u).start()
    for t in range(2):
        for u in step:
            for i in range(3):
                ag_line(t, i, u).start()
        for i in range(3):
            ag_own(t, i).start()
    for i in range(3):
        for u in step:
            ids_line(i, u).wait_recv()
        ids_pass(i).start()
    for i in range(3):
        ids_own(i).wait_recv()
        ids_pass(i).wait_recv()

    before = (lax.broadcasted_iota(jnp.int32, (TOK, TOK), 0) < lax.broadcasted_iota(jnp.int32, (TOK, TOK), 1))
    before = jnp.where(before, 1.0, 0.0).astype(BF)
    line = lax.broadcasted_iota(jnp.int32, (32, TOK), 0)
    for i in range(3):
        ax_a, ax_b, ax_c = AXES[i]
        shift = [0, 0, 0]
        shift[ax_b] = (line >> 2) & 3
        shift[ax_c] = line & 3
        at = [(zyx[n] + shift[n]) & 3 for n in range(3)]
        expert = ((((at[0] * 4 + at[1]) * 4 + at[2]) * 2 + core) * 2 + (line >> 4)).astype(F32)
        for u in range(4):
            for c in range(2):
                s = u * 2 + c
                named = jnp.zeros((32, TOK), F32)
                weight = jnp.zeros((32, TOK), F32)
                for k in range(TOPK):
                    same = ids[i, u, c, k:k + 1, :] == expert
                    named = named + jnp.where(same, 1.0, 0.0)
                    weight = weight + jnp.where(same, ids[i, u, c, TOPK + k:TOPK + k + 1, :], 0.0)
                rank = dot(named.astype(BF), before, NN)
                place = jnp.where(named > 0.5, rank + float(s * CAP), -1.0)
                for e in range(2):
                    key[i, e, :, s * TOK:(s + 1) * TOK] = place[e * 16:(e + 1) * 16]
                    gate[i, e, :, s * TOK:(s + 1) * TOK] = weight[e * 16:(e + 1) * 16]

    slot = lax.broadcasted_iota(jnp.int32, (ROWS, 8 * TOK), 0).astype(F32)

    def build_pick(i, e, weighted):
        def one(n, carry):
            same = key[i, e, pl.ds(n, 1), :] == slot
            value = gate[i, e, pl.ds(n, 1), :] if weighted else 1.0
            pick[n] = jnp.where(same, value, 0.0).astype(BF)
            return carry

        lax.fori_loop(0, 16, one, 0)

    def dispatch(t, i, e):
        width = PARTS[i][1]
        build_pick(i, e, t == 1)

        def half(h, carry):
            rows = pick[pl.ds(h * 8, 8)].reshape(8 * ROWS, 8 * TOK)
            value = dot(rows, near[i][...].reshape(8 * TOK, width), NN).astype(BF)
            send[i][e, pl.ds(2 * h, 2)] = value.reshape(2, 4, ROWS, width)
            return carry

        lax.fori_loop(0, 2, half, 0)
        got[t][i][e, 0, 0] = send[i][e, 0, 0]
        for r in step:
            b1(t, i, e, r).start()
        for r in step:
            c0(t, i, e, r).start()
        for r in step:
            b0(t, i, e, r).start()

    def forward(t, e):
        for i in range(3):
            for r in step:
                b1(t, i, e, r).wait_recv()
            for q in step:
                c1(t, i, e, q).start()

    def arrived(t, i, e):
        for r in step:
            b0(t, i, e, r).wait_recv()
            c0(t, i, e, r).wait_recv()
            c1(t, i, e, r).wait_recv()

    def sends_done(t, i, e):
        for r in step:
            b0(t, i, e, r).wait_send()
            b1(t, i, e, r).wait_send()
            c0(t, i, e, r).wait_send()

    def in_order(t, i, e):
        width = PARTS[i][1]

        def half(h, carry):
            rows = pl.ds(pl.multiple_of(h * 384, 384), 384)
            tmp[rows, :] = dot(perm[i - 1, rows, :], got[t][i][e].reshape(16 * ROWS, width), NN).astype(BF)
            return carry

        lax.fori_loop(0, 2, half, 0)
        got[t][i][e] = tmp[...].reshape(4, 4, ROWS, width)

    def each(count, body):
        lax.fori_loop(0, count, lambda n, c: (body(n), c)[1], 0)

    def gather_pass(t):
        for i in range(3):
            for u in step:
                ag_line(t, i, u).wait_recv()
                ag_pass(t, i, u).start()

    def gather_end(t, i):
        ag_own(t, i).wait_recv()
        for u in step:
            ag_pass(t, i, u).wait_recv()
            ag_pass(t, i, u).wait_send()
            ag_line(t, i, u).wait_send()
        ag_own(t, i).wait_send()
        ag_self(t, i).wait()

    gather_pass(0)
    for i in range(3):
        gather_end(0, i)
        each(2, lambda e: dispatch(0, i, e))
    gather_pass(1)
    each(2, lambda e: forward(0, e))

    for i in range(3):
        gather_end(1, i)
        refill(i).start()
    for i in range(3):
        refill(i).wait()

    def dispatch_dy(e):
        for i in range(3):
            sends_done(0, i, e)
            dispatch(1, i, e)

    each(2, dispatch_dy)

    load_p.wait()

    def halves(t, i, e, h):
        return got[t][i][e, pl.ds(2 * h, 2)].reshape(8 * ROWS, PARTS[i][1])

    def first(e):
        for i in range(3):
            arrived(0, i, e)
        for i in (1, 2):
            in_order(0, i, e)
        load_w(0, e).wait()
        load_w(1, e).wait()

        def half(h):
            for n in range(2):
                total = dot(halves(0, 0, e, h), wbuf[n][0:768], NN)
                for i in (1, 2):
                    total = total + dot(halves(0, i, e, h), wbuf[n][PARTS[i][0]:PARTS[i][0] + PARTS[i][1]], NN)
                pre[e, n, pl.ds(pl.multiple_of(h * 384, 384), 384)] = total

        each(2, half)
        load_w(0, 1 - e).start()
        load_w(1, 1 - e).start()
        forward(1, e)

    each(2, first)

    def second(e):
        for i in range(3):
            arrived(1, i, e)
        for i in (1, 2):
            in_order(1, i, e)
        for n in range(3):
            load_w(n, e).wait()

        def half(h):
            grad = dot(halves(1, 0, e, h), wbuf[2][:, 0:768], NT)
            for i in (1, 2):
                grad = grad + dot(halves(1, i, e, h), wbuf[2][:, PARTS[i][0]:PARTS[i][0] + PARTS[i][1]], NT)
            rows = pl.ds(pl.multiple_of(h * 384, 384), 384)
            pre_gate = pre[e, 0, rows]
            pre_up = pre[e, 1, rows]
            sig = jax.nn.sigmoid(pre_gate)
            silu = pre_gate * sig
            act[e, 0, rows] = (silu * pre_up).astype(BF)
            act[e, 1, rows] = (grad * pre_up * sig * (1.0 + pre_gate * (1.0 - sig))).astype(BF)
            act[e, 2, rows] = (grad * silu).astype(BF)

        each(2, half)
        for i in range(3):
            sends_done(1, i, e)
            start, width = PARTS[i]
            if i > 0:
                def turn(h):
                    rows = pl.ds(pl.multiple_of(h * 384, 384), 384)
                    for n in range(2):
                        turned[n, rows] = dot(perm[2 - i, rows, :], act[e, 1 + n], NN).astype(BF)

                each(2, turn)

            def part(h):
                rows = pl.ds(pl.multiple_of(h * 384, 384), 384)
                left = act[e, 1, rows] if i == 0 else turned[0, rows]
                right = act[e, 2, rows] if i == 0 else turned[1, rows]
                total = dot(left, wbuf[0][start:start + width], NT) + dot(right, wbuf[1][start:start + width], NT)
                send[i][e, pl.ds(2 * h, 2)] = total.astype(BF).reshape(2, 4, ROWS, width)

            each(2, part)
            back[i][e, 0, 0] = send[i][e, 0, 0]
            for q in step:
                rc1(i, e, q).start()
            for q in step:
                rb0(i, e, q).start()
            for q in step:
                rc0(i, e, q).start()

        @pl.when(e == 0)
        def _():
            for n in range(3):
                load_w(n, 1).start()

    each(2, second)

    def send_on(e):
        for i in range(3):
            for q in step:
                rc1(i, e, q).wait_recv()
            for r in step:
                rb1(i, e, r).start()

    def weight_grads(e):
        @pl.when(e == 1)
        def _():
            for n in range(3):
                store_w(n, 0).wait()

        for i in range(3):
            start, width = PARTS[i]
            rows_x = got[0][i][e].reshape(16 * ROWS, width)
            rows_dy = got[1][i][e].reshape(16 * ROWS, width)
            wbuf[0][start:start + width] = dot(rows_x, act[e, 1], TN).astype(BF)
            wbuf[1][start:start + width] = dot(rows_x, act[e, 2], TN).astype(BF)
            wbuf[2][:, start:start + width] = dot(act[e, 0], rows_dy, TN).astype(BF)
        for n in range(3):
            store_w(n, e).start()

    def collect(e):
        for i in range(3):
            width = PARTS[i][1]
            for r in step:
                rb0(i, e, r).wait_recv()
                rc0(i, e, r).wait_recv()
                rb1(i, e, r).wait_recv()
            build_pick(i, e, False)

            def block(u):
                rows = pick[:, :, pl.ds(pl.multiple_of(u * 256, 256), 256)].reshape(16 * ROWS, 256)
                total = dot(rows, back[i][e].reshape(16 * ROWS, width), TN).reshape(2, TOK, width)
                held = near[i][u].astype(F32)
                near[i][u] = jnp.where(e == 0, total, total + held).astype(BF)

            each(4, block)

            @pl.when(e == 1)
            def _():
                z_sib(i).start()

    def tail(e):
        send_on(e)
        weight_grads(e)

    each(2, tail)
    each(2, collect)

    for i in range(3):
        z_sib(i).wait_recv()
        z_sib(i).wait_send()
        for u in step:
            near[i][u, core] = (near[i][u, core].astype(F32) + from_sib[i][u].astype(F32)).astype(BF)
            z_line(i, u).start()
    for i in range(3):
        total = near[i][0, core].astype(F32) + from_sib[i][0].astype(F32)
        for u in step:
            z_line(i, u).wait_recv()
            total = total + last[i][u - 1].astype(F32)
        out_t[:, PARTS[i][0]:PARTS[i][0] + PARTS[i][1]] = total.astype(BF)

    for n in range(3):
        store_w(n, 1).wait()
    for i in range(3):
        for u in step:
            z_line(i, u).wait_send()
            ids_line(i, u).wait_send()
        ids_own(i).wait_send()
        ids_pass(i).wait_send()

    def drain(e):
        for i in range(3):
            for r in step:
                c1(0, i, e, r).wait_send()
                c1(1, i, e, r).wait_send()
                rc0(i, e, r).wait_send()
                rc1(i, e, r).wait_send()
                rb0(i, e, r).wait_send()
                rb1(i, e, r).wait_send()

    each(2, drain)


def per_device(tokens, out_grad, expert_ids, gate_vals, w_gate, w_up, w_down):
    width = tokens.shape[1]
    info = jnp.concatenate(
        [expert_ids.T.astype(F32), gate_vals.T, jnp.zeros((24 - 2 * TOPK, TOK), F32)], axis=0
    )
    row = jnp.arange(16 * ROWS)
    block, inner = row // 12, row % 12
    hi, mid, lo = block // 16, (block // 4) % 4, block % 4
    at = jnp.stack([(lo * 16 + hi * 4 + mid) * 12 + inner, (mid * 16 + lo * 4 + hi) * 12 + inner])
    perm = (at[:, :, None] == row[None, None, :]).astype(BF)

    any_ = pl.BlockSpec(memory_space=pl.ANY)
    vmem = pl.BlockSpec(memory_space=pltpu.VMEM)
    widths = [p[1] for p in PARTS]
    hbm_shapes = [jax.ShapeDtypeStruct((4, 2, TOK, c), BF) for c in widths]
    for _ in range(3):
        hbm_shapes += [jax.ShapeDtypeStruct((2, 3, 3, ROWS, c), BF) for c in widths]
    scratch = [pltpu.VMEM((4, 2, TOK, c), BF) for c in widths]
    for _ in range(4):
        scratch += [pltpu.VMEM((2, 4, 4, ROWS, c), BF) for c in widths]
    scratch += [pltpu.VMEM((4, TOK, c), BF) for c in widths]
    scratch += [pltpu.VMEM((3, TOK, c), BF) for c in widths]
    dma = pltpu.SemaphoreType.DMA
    scratch += [
        pltpu.VMEM((3, 4, 2, 24, TOK), F32),
        pltpu.VMEM((3, 2, 16, 8 * TOK), F32),
        pltpu.VMEM((3, 2, 16, 8 * TOK), F32),
        pltpu.VMEM((16, ROWS, 8 * TOK), BF),
        pltpu.VMEM((2, 16 * ROWS, 16 * ROWS), BF),
        pltpu.VMEM((16 * ROWS, 640), BF),
        pltpu.VMEM((2, 3, 16 * ROWS, HID), BF),
        pltpu.VMEM((2, 2, 16 * ROWS, HID), F32),
        pltpu.VMEM((2, 16 * ROWS, HID), BF),
        (pltpu.VMEM((width, HID), BF), pltpu.VMEM((width, HID), BF), pltpu.VMEM((HID, width), BF)),
        dma((3, 4)),
        dma((3, 5)), dma((3, 5)),
        dma((2, 3, 7)), dma((2, 3, 7)),
        dma((2, 3, 2, 12)), dma((2, 3, 2, 12)),
        dma((3, 2, 12)), dma((3, 2, 12)),
        dma((3, 4)), dma((3, 4)),
        dma((3,)), dma((3,)),
    ]
    results = pl.pallas_call(
        kernel,
        out_shape=[
            jax.ShapeDtypeStruct(tokens.shape, BF),
            jax.ShapeDtypeStruct(w_gate.shape, BF),
            jax.ShapeDtypeStruct(w_up.shape, BF),
            jax.ShapeDtypeStruct(w_down.shape, BF),
        ] + hbm_shapes,
        in_specs=[vmem] + [any_] * 6,
        out_specs=[vmem] + [any_] * (3 + len(hbm_shapes)),
        scratch_shapes=scratch,
        compiler_params=pltpu.CompilerParams(collective_id=0, has_side_effects=True, vmem_limit_bytes=63 * 10**6),
        cost_estimate=pl.CostEstimate(flops=60 * 10**9, bytes_accessed=60 * 10**6, transcendentals=10**6),
    )(info, tokens, out_grad, perm, w_gate, w_up, w_down)
    return tuple(results[:4])


def solution(mesh):
    rows = P(("group", "member"), None)
    whole = P(("group", "member"), None, None)
    return jax.shard_map(
        per_device,
        mesh=mesh,
        in_specs=(rows, rows, rows, rows, whole, whole, whole),
        out_specs=(rows, whole, whole, whole),
        check_vma=False,
    )
```

profile of v0, /device:TPU:0, one launch (start us, length us, event | category | flops | bytes accessed | tf_op | source)
XLA Modules:
  0.0 212.1 jit_solution(10271602659415597865)
XLA Ops:
  0.6 0.1 pad.4.clone
  0.7 0.1 multiply_add_fusion
  0.8 0.7 convert_bitcast_fusion
  1.5 1.4 maximum_maximum_fusion.info
  2.9 1.9 fusion.perm_in
  4.7 195.2 %shard_map.102 = (bf16[128,2048]{1,0:T(8,128)(2,1)}, bf16[2,2048,512]{2,1,0:T(8,128)(2,1)}, bf16[2,2048,512]{2,1,0:T(8,128)(2,1)}, bf16[2,512,2048]{2,1,0:T(8,12...) custom-call(f32[24,128]{1,0:T(8,128)} %maximum_maximum_fusion.info, ...), custom_call_target="tpu_custom_call" | custom-call | flops 60000002048 | bytes 60000000 | tf_op jit(solution)/shard_map/pallas_call | solution.py:508
  199.9 1.9 copy.15
  201.8 0.0 copy-start.1
  201.8 4.6 %copy.16 = bf16[2,2048,512]{2,1,0:T(8,128)(2,1)} copy(bf16[2,2048,512]{2,1,0:T(8,128)(2,1)} %get-tuple-element.19) | data formatting | bytes 8388608
  206.4 0.0 copy-done.1
  206.4 0.0 copy-start
  206.4 2.1 %copy.17 = bf16[2,2048,512]{2,1,0:T(8,128)(2,1)} copy(bf16[2,2048,512]{2,1,0:T(8,128)(2,1)S(1)} %copy-done.1) | data formatting | bytes 8388608
  208.6 1.6 copy-done
  210.1 2.0 copy.18
  (2 shorter events, 0.0 us)
Async XLA Ops:
  201.8 4.6 %copy-start.1 = (bf16[2,2048,512]{2,1,0:T(8,128)(2,1)S(1)}, bf16[2,2048,512]{2,1,0:T(8,128)(2,1)}, u32[]{:S(2)}) copy-start(bf16[2,2048,512]{2,1,0:T(8,128)(2,1)} %get-tuple-element.20) | copy-start | bytes 12582916
  206.4 3.7 %copy-start = (bf16[2,512,2048]{2,1,0:T(8,128)(2,1)S(1)}, bf16[2,512,2048]{2,1,0:T(8,128)(2,1)}, u32[]{:S(2)}) copy-start(bf16[2,512,2048]{2,1,0:T(8,128)(2,1)} %get-tuple-element.21) | copy-start | bytes 12582916
where the time goes:
time: 213 us; the launch traced here: 212 us
  Pallas kernels  195 us (92%)
  local copies, waits for them, and re-layouts  12.3 us (6%)
  other arithmetic  4 us (2%)
    pallas_call x1, Pallas kernels, per_device(): pl.pallas_call(kernel, out_shape=[jax.ShapeDtypeStruct(tokens.shape, BF),...  195 us
    unnamed x8, local copies, waits for them, and re-layouts  12.2 us

commit v1 on v0

--- a/solution.py
+++ b/solution.py
@@ -26,12 +26,12 @@
 TN = ((0,), (0,))
 
 
-def kernel(info, tok, dy, perm_in, wg, wu, wd, out_t, out_g, out_u, out_d, *rest):
+def kernel(ids_in, gates_in, tok, dy, wg, wu, wd, out_t, out_g, out_u, out_d, *rest):
     hold_dy, relay = rest[0:3], (rest[3:6], rest[6:9], rest[9:12])
     rest = rest[12:]
     near, send, got = rest[0:3], rest[3:6], (rest[6:9], rest[9:12])
     back, from_sib, last = rest[12:15], rest[15:18], rest[18:21]
-    (ids, key, gate, pick, perm, tmp, act, pre, turned, wbuf, loc, ids_s, ids_r, ag_s, ag_r, d_s, d_r, b_s, b_r, z_s,
+    (info, ids, key, gate, pick, perm, tmp, act, pre, turned, wbuf, loc, ids_s, ids_r, ag_s, ag_r, d_s, d_r, b_s, b_r, z_s,
      z_r, w_sem, o_sem) = rest[21:]
 
     g = lax.axis_index("group")
@@ -78,11 +78,16 @@
         part = gathered[t][i].at[u, core]
         return remote(part, part, ag_s.at[t, i, 3 + u], ag_r.at[t, i, 3 + u], sib)
 
-    def ag_self(t, i):
-        return pltpu.make_async_copy(source[t].at[:, cols(i)], gathered[t][i].at[0, core], loc.at[t, i])
+    def ag_self(i):
+        return pltpu.make_async_copy(tok.at[:, cols(i)], near[i].at[0, core], loc.at[0, i])
 
     def refill(i):
-        return pltpu.make_async_copy(hold_dy[i], near[i], loc.at[2, i])
+        far, own = pl.ds(1, 3), 1 - core
+        return (
+            pltpu.make_async_copy(hold_dy[i].at[far], near[i].at[far], loc.at[1, i]),
+            pltpu.make_async_copy(hold_dy[i].at[0, own], near[i].at[0, own], loc.at[2, i]),
+            pltpu.make_async_copy(dy.at[:, cols(i)], near[i].at[0, core], loc.at[3, i]),
+        )
 
     def b0(t, i, e, r):
         k = r - 1
@@ -120,11 +125,11 @@
         return remote(relay[2][i].at[e, :, r - 1], back[i].at[e, r, pl.ds(1, 3)], b_s.at[i, e, k], b_r.at[i, e, k],
                       peer(AXES[i][1], -r))
 
-    def z_sib(i):
-        return remote(near[i].at[:, 1 - core], from_sib[i], z_s.at[i, 0], z_r.at[i, 0], sib)
+    def z_sib(i, u):
+        return remote(near[i].at[u, 1 - core], from_sib[i].at[u], z_s.at[i, u], z_r.at[i, u], sib)
 
     def z_line(i, u):
-        return remote(near[i].at[u, core], last[i].at[u - 1], z_s.at[i, u], z_r.at[i, u], peer(AXES[i][0], -u))
+        return remote(near[i].at[u, core], last[i].at[u - 1], z_s.at[i, 3 + u], z_r.at[i, 3 + u], peer(AXES[i][0], -u))
 
     weights = (wg, wu, wd)
 
@@ -145,11 +150,11 @@
     pl.semaphore_signal(barrier, inc=1, device_id=sib, device_id_type=MESH)
     for n in range(3):
         load_w(n, 0).start()
-    load_p = pltpu.make_async_copy(perm_in, perm, loc.at[2, 3])
-    load_p.start()
-    for i in range(3):
-        ag_self(0, i).start()
-        ag_self(1, i).start()
+    info[...] = jnp.zeros((32, TOK), F32)
+    info[0:TOPK] = ids_in[...].astype(F32)
+    info[16:16 + TOPK] = gates_in[...]
+    for i in range(3):
+        ag_self(i).start()
         ids[i, 0, core] = info[...]
     pl.semaphore_wait(barrier, 10)
 
@@ -157,16 +162,49 @@
         ids_own(i).start()
         for u in step:
             ids_line(i, u).start()
-    for t in range(2):
-        for u in step:
+
+    def gather_start(t):
+        for u in (1, 3, 2):
             for i in range(3):
                 ag_line(t, i, u).start()
         for i in range(3):
             ag_own(t, i).start()
+
+    def gather_pass(t):
+        for u in (1, 3, 2):
+            for i in range(3):
+                ag_line(t, i, u).wait_recv()
+                ag_pass(t, i, u).start()
+
+    def gather_end(t, i):
+        ag_own(t, i).wait_recv()
+        for u in (1, 2, 3):
+            ag_pass(t, i, u).wait_recv()
+            ag_pass(t, i, u).wait_send()
+            ag_line(t, i, u).wait_send()
+        ag_own(t, i).wait_send()
+
+    gather_start(0)
+    gather_start(1)
     for i in range(3):
         for u in step:
             ids_line(i, u).wait_recv()
         ids_pass(i).start()
+
+    def build_perm(n, carry):
+        row = lax.broadcasted_iota(jnp.int32, (192, TOK), 0) + n * 192
+        group = (row * 5462) >> 16
+        inner = row - group * 12
+        hi, mid, lo = group >> 4, (group >> 2) & 3, group & 3
+        rows = pl.ds(pl.multiple_of(n * 192, 192), 192)
+        lane = lax.broadcasted_iota(jnp.int32, (192, TOK), 1)
+        for way, target in enumerate((lo * 16 + hi * 4 + mid, mid * 16 + lo * 4 + hi)):
+            ahead = target * 12 + inner - lane
+            for c in range(6):
+                perm[way, rows, c * TOK:(c + 1) * TOK] = jnp.where(ahead == c * TOK, 1.0, 0.0).astype(BF)
+        return carry
+
+    lax.fori_loop(0, 4, build_perm, 0)
     for i in range(3):
         ids_own(i).wait_recv()
         ids_pass(i).wait_recv()
@@ -189,7 +227,7 @@
                 for k in range(TOPK):
                     same = ids[i, u, c, k:k + 1, :] == expert
                     named = named + jnp.where(same, 1.0, 0.0)
-                    weight = weight + jnp.where(same, ids[i, u, c, TOPK + k:TOPK + k + 1, :], 0.0)
+                    weight = weight + jnp.where(same, ids[i, u, c, 16 + k:17 + k, :], 0.0)
                 rank = dot(named.astype(BF), before, NN)
                 place = jnp.where(named > 0.5, rank + float(s * CAP), -1.0)
                 for e in range(2):
@@ -198,11 +236,16 @@
 
     slot = lax.broadcasted_iota(jnp.int32, (ROWS, 8 * TOK), 0).astype(F32)
 
-    def build_pick(i, e, weighted):
+    def build_pick(i, e, weighted, keep=False):
         def one(n, carry):
             same = key[i, e, pl.ds(n, 1), :] == slot
             value = gate[i, e, pl.ds(n, 1), :] if weighted else 1.0
-            pick[n] = jnp.where(same, value, 0.0).astype(BF)
+            picked = jnp.where(same, value, 0.0).astype(BF)
+            if keep:
+                for half in range(2):
+                    got[1][i][half, n // 4, lax.rem(n, 4), :, 0:512] = picked[:, half * 512:half * 512 + 512]
+            else:
+                pick[n] = picked
             return carry
 
         lax.fori_loop(0, 16, one, 0)
@@ -230,7 +273,8 @@
         for i in range(3):
             for r in step:
                 b1(t, i, e, r).wait_recv()
-            for q in step:
+        for q in (1, 3, 2):
+            for i in range(3):
                 c1(t, i, e, q).start()
 
     def arrived(t, i, e):
@@ -259,33 +303,26 @@
     def each(count, body):
         lax.fori_loop(0, count, lambda n, c: (body(n), c)[1], 0)
 
-    def gather_pass(t):
-        for i in range(3):
-            for u in step:
-                ag_line(t, i, u).wait_recv()
-                ag_pass(t, i, u).start()
-
-    def gather_end(t, i):
-        ag_own(t, i).wait_recv()
-        for u in step:
-            ag_pass(t, i, u).wait_recv()
-            ag_pass(t, i, u).wait_send()
-            ag_line(t, i, u).wait_send()
-        ag_own(t, i).wait_send()
-        ag_self(t, i).wait()
-
     gather_pass(0)
     for i in range(3):
         gather_end(0, i)
-        each(2, lambda e: dispatch(0, i, e))
+        ag_self(i).wait()
+
+    def dispatch_tok(e):
+        for i in range(3):
+            dispatch(0, i, e)
+
+    each(2, dispatch_tok)
     gather_pass(1)
     each(2, lambda e: forward(0, e))
 
     for i in range(3):
         gather_end(1, i)
-        refill(i).start()
-    for i in range(3):
-        refill(i).wait()
+        for one in refill(i):
+            one.start()
+    for i in range(3):
+        for one in refill(i):
+            one.wait()
 
     def dispatch_dy(e):
         for i in range(3):
@@ -293,8 +330,6 @@
             dispatch(1, i, e)
 
     each(2, dispatch_dy)
-
-    load_p.wait()
 
     def halves(t, i, e, h):
         return got[t][i][e, pl.ds(2 * h, 2)].reshape(8 * ROWS, PARTS[i][1])
@@ -308,11 +343,19 @@
         load_w(1, e).wait()
 
         def half(h):
+            both = []
             for n in range(2):
                 total = dot(halves(0, 0, e, h), wbuf[n][0:768], NN)
                 for i in (1, 2):
                     total = total + dot(halves(0, i, e, h), wbuf[n][PARTS[i][0]:PARTS[i][0] + PARTS[i][1]], NN)
-                pre[e, n, pl.ds(pl.multiple_of(h * 384, 384), 384)] = total
+                both.append(total)
+            pre_gate, pre_up = both
+            rows = pl.ds(pl.multiple_of(h * 384, 384), 384)
+            sig = jax.nn.sigmoid(pre_gate)
+            silu = pre_gate * sig
+            act[e, 0, rows] = (silu * pre_up).astype(BF)
+            pre[e, 0, rows] = pre_up * sig * (1.0 + pre_gate * (1.0 - sig))
+            pre[e, 1, rows] = silu
 
         each(2, half)
         load_w(0, 1 - e).start()
@@ -334,13 +377,8 @@
             for i in (1, 2):
                 grad = grad + dot(halves(1, i, e, h), wbuf[2][:, PARTS[i][0]:PARTS[i][0] + PARTS[i][1]], NT)
             rows = pl.ds(pl.multiple_of(h * 384, 384), 384)
-            pre_gate = pre[e, 0, rows]
-            pre_up = pre[e, 1, rows]
-            sig = jax.nn.sigmoid(pre_gate)
-            silu = pre_gate * sig
-            act[e, 0, rows] = (silu * pre_up).astype(BF)
-            act[e, 1, rows] = (grad * pre_up * sig * (1.0 + pre_gate * (1.0 - sig))).astype(BF)
-            act[e, 2, rows] = (grad * silu).astype(BF)
+            act[e, 1, rows] = (grad * pre[e, 0, rows]).astype(BF)
+            act[e, 2, rows] = (grad * pre[e, 1, rows]).astype(BF)
 
         each(2, half)
         for i in range(3):
@@ -381,7 +419,8 @@
         for i in range(3):
             for q in step:
                 rc1(i, e, q).wait_recv()
-            for r in step:
+        for r in (1, 3, 2):
+            for i in range(3):
                 rb1(i, e, r).start()
 
     def weight_grads(e):
@@ -400,42 +439,56 @@
         for n in range(3):
             store_w(n, e).start()
 
-    def collect(e):
-        for i in range(3):
-            width = PARTS[i][1]
-            for r in step:
-                rb0(i, e, r).wait_recv()
-                rc0(i, e, r).wait_recv()
-                rb1(i, e, r).wait_recv()
-            build_pick(i, e, False)
-
-            def block(u):
-                rows = pick[:, :, pl.ds(pl.multiple_of(u * 256, 256), 256)].reshape(16 * ROWS, 256)
-                total = dot(rows, back[i][e].reshape(16 * ROWS, width), TN).reshape(2, TOK, width)
-                held = near[i][u].astype(F32)
-                near[i][u] = jnp.where(e == 0, total, total + held).astype(BF)
-
-            each(4, block)
-
-            @pl.when(e == 1)
-            def _():
-                z_sib(i).start()
+    def returned(i, e):
+        for r in step:
+            rb0(i, e, r).wait_recv()
+            rc0(i, e, r).wait_recv()
+            rb1(i, e, r).wait_recv()
+
+    def collect(i):
+        width = PARTS[i][1]
+        build_pick(i, 0, False)
+        returned(i, 0)
+        for u in range(4):
+            rows = pick[:, :, u * 256:(u + 1) * 256].reshape(16 * ROWS, 256)
+            total = dot(rows, back[i][0].reshape(16 * ROWS, width), TN).reshape(2, TOK, width)
+            near[i][u] = total.astype(BF)
+
+    def collect_last(i, u):
+        width = PARTS[i][1]
+        lanes = (u % 2) * 256
+        rows = got[1][i][u // 2, :, :, :, lanes:lanes + 256].reshape(16 * ROWS, 256)
+        total = dot(rows, back[i][1].reshape(16 * ROWS, width), TN).reshape(2, TOK, width)
+        near[i][u] = (total + near[i][u].astype(F32)).astype(BF)
+        z_sib(i, u).start()
+
+    def both(i, u):
+        z_sib(i, u).wait_recv()
+        return near[i][u, core].astype(F32) + from_sib[i][u].astype(F32)
+
+    def line_out(i, u):
+        near[i][u, core] = both(i, u).astype(BF)
+        z_line(i, u).start()
 
     def tail(e):
         send_on(e)
         weight_grads(e)
 
     each(2, tail)
-    each(2, collect)
-
-    for i in range(3):
-        z_sib(i).wait_recv()
-        z_sib(i).wait_send()
-        for u in step:
-            near[i][u, core] = (near[i][u, core].astype(F32) + from_sib[i][u].astype(F32)).astype(BF)
-            z_line(i, u).start()
-    for i in range(3):
-        total = near[i][0, core].astype(F32) + from_sib[i][0].astype(F32)
+    for i in range(3):
+        collect(i)
+    for i in range(3):
+        build_pick(i, 1, False, True)
+    for i in range(3):
+        returned(i, 1)
+        collect_last(i, 2)
+    for n, u in enumerate((1, 3, 0)):
+        for i in range(3):
+            collect_last(i, u)
+        for i in range(3):
+            line_out(i, (2, 1, 3)[n])
+    for i in range(3):
+        total = both(i, 0)
         for u in step:
             z_line(i, u).wait_recv()
             total = total + last[i][u - 1].astype(F32)
@@ -444,6 +497,8 @@
     for n in range(3):
         store_w(n, 1).wait()
     for i in range(3):
+        for u in range(4):
+            z_sib(i, u).wait_send()
         for u in step:
             z_line(i, u).wait_send()
             ids_line(i, u).wait_send()
@@ -463,17 +518,39 @@
     each(2, drain)
 
 
+def copy_kernel(*refs):
+    src, dst, held, sems = refs[:4], refs[4:8], refs[8:12], refs[12]
+    moves = [(0, (pl.ds(0, TOK),))]
+    for k in range(8):
+        for n in (1, 2, 3):
+            size = src[n].shape[1] // 4
+            moves.append((n, (k // 4, pl.ds((k % 4) * size, size))))
+    into = [pltpu.make_async_copy(src[n].at[at], held[n].at[at], sems.at[0, j]) for j, (n, at) in enumerate(moves)]
+    out = [pltpu.make_async_copy(held[n].at[at], dst[n].at[at], sems.at[1, j]) for j, (n, at) in enumerate(moves)]
+    for one in into:
+        one.start()
+    for one, other in zip(into, out):
+        one.wait()
+        other.start()
+    for one in out:
+        one.wait()
+
+
+def hand_over(*arrays):
+    any_ = pl.BlockSpec(memory_space=pl.ANY)
+    return pl.pallas_call(
+        copy_kernel,
+        out_shape=[jax.ShapeDtypeStruct(a.shape, a.dtype) for a in arrays],
+        in_specs=[any_] * 4,
+        out_specs=[any_] * 4,
+        scratch_shapes=[pltpu.VMEM(a.shape, a.dtype) for a in arrays] + [pltpu.SemaphoreType.DMA((2, 25))],
+        compiler_params=pltpu.CompilerParams(vmem_limit_bytes=63 * 10**6),
+        cost_estimate=pl.CostEstimate(flops=0, bytes_accessed=26 * 10**6, transcendentals=0),
+    )(*arrays)
+
+
 def per_device(tokens, out_grad, expert_ids, gate_vals, w_gate, w_up, w_down):
     width = tokens.shape[1]
-    info = jnp.concatenate(
-        [expert_ids.T.astype(F32), gate_vals.T, jnp.zeros((24 - 2 * TOPK, TOK), F32)], axis=0
-    )
-    row = jnp.arange(16 * ROWS)
-    block, inner = row // 12, row % 12
-    hi, mid, lo = block // 16, (block // 4) % 4, block % 4
-    at = jnp.stack([(lo * 16 + hi * 4 + mid) * 12 + inner, (mid * 16 + lo * 4 + hi) * 12 + inner])
-    perm = (at[:, :, None] == row[None, None, :]).astype(BF)
-
     any_ = pl.BlockSpec(memory_space=pl.ANY)
     vmem = pl.BlockSpec(memory_space=pltpu.VMEM)
     widths = [p[1] for p in PARTS]
@@ -487,7 +564,8 @@
     scratch += [pltpu.VMEM((3, TOK, c), BF) for c in widths]
     dma = pltpu.SemaphoreType.DMA
     scratch += [
-        pltpu.VMEM((3, 4, 2, 24, TOK), F32),
+        pltpu.VMEM((32, TOK), F32),
+        pltpu.VMEM((3, 4, 2, 32, TOK), F32),
         pltpu.VMEM((3, 2, 16, 8 * TOK), F32),
         pltpu.VMEM((3, 2, 16, 8 * TOK), F32),
         pltpu.VMEM((16, ROWS, 8 * TOK), BF),
@@ -497,12 +575,12 @@
         pltpu.VMEM((2, 2, 16 * ROWS, HID), F32),
         pltpu.VMEM((2, 16 * ROWS, HID), BF),
         (pltpu.VMEM((width, HID), BF), pltpu.VMEM((width, HID), BF), pltpu.VMEM((HID, width), BF)),
-        dma((3, 4)),
+        dma((4, 3)),
         dma((3, 5)), dma((3, 5)),
         dma((2, 3, 7)), dma((2, 3, 7)),
         dma((2, 3, 2, 12)), dma((2, 3, 2, 12)),
         dma((3, 2, 12)), dma((3, 2, 12)),
-        dma((3, 4)), dma((3, 4)),
+        dma((3, 7)), dma((3, 7)),
         dma((3,)), dma((3,)),
     ]
     results = pl.pallas_call(
@@ -513,13 +591,13 @@
             jax.ShapeDtypeStruct(w_up.shape, BF),
             jax.ShapeDtypeStruct(w_down.shape, BF),
         ] + hbm_shapes,
-        in_specs=[vmem] + [any_] * 6,
+        in_specs=[vmem, vmem] + [any_] * 5,
         out_specs=[vmem] + [any_] * (3 + len(hbm_shapes)),
         scratch_shapes=scratch,
         compiler_params=pltpu.CompilerParams(collective_id=0, has_side_effects=True, vmem_limit_bytes=63 * 10**6),
         cost_estimate=pl.CostEstimate(flops=60 * 10**9, bytes_accessed=60 * 10**6, transcendentals=10**6),
-    )(info, tokens, out_grad, perm, w_gate, w_up, w_down)
-    return tuple(results[:4])
+    )(expert_ids.T, gate_vals.T, tokens, out_grad, w_gate, w_up, w_down)
+    return hand_over(*results[:4])
 
 
 def solution(mesh):

time: 213 us -> 202 us (0.948)
  local copies, waits for them, and re-layouts: 12.3 us -> 0 us
  Pallas kernels: 195 us -> 201 us
  other arithmetic: 4 us -> 0 us
    unnamed x8 -> x0, local copies, waits for them, and re-layouts: 12.2 us -> none
    pallas_call x0 -> x1, Pallas kernels: none -> 9.93 us  [hand_over(): pl.pallas_call(copy_kernel, out_shape=[jax.ShapeDtypeStruct(a.shape, a.dt...]
    pallas_call x1, Pallas kernels: 195 us -> 191 us  [per_device(): pl.pallas_call(kernel, out_shape=[jax.ShapeDtypeStruct(tokens.shape, BF),...]
    convert_element_type x2 -> x0, other arithmetic: 2.55 us -> none  [the longest x1 1.85 us: per_device(): perm = (at[:, :, None] == row[None, None, :]).astype(BF)]
where the time goes in v1:
time: 202 us
  Pallas kernels  201 us (100%)
    pallas_call x1, Pallas kernels, per_device(): pl.pallas_call(kernel, out_shape=[jax.ShapeDtypeStruct(tokens.shape, BF),...  191 us
    pallas_call x1, Pallas kernels, hand_over(): pl.pallas_call(copy_kernel, out_shape=[jax.ShapeDtypeStruct(a.shape, a.dt...  9.93 us

profile of v1, /device:TPU:0, one launch (start us, length us, event | category | flops | bytes accessed | tf_op | source)
XLA Modules:
  0.0 201.9 jit_solution(15316671140869484276)
XLA Ops:
  0.6 191.2 %shard_map.102 = (bf16[128,2048]{1,0:T(8,128)(2,1)}, bf16[2,2048,512]{2,1,0:T(8,128)(2,1)}, bf16[2,2048,512]{2,1,0:T(8,128)(2,1)}, bf16[2,512,2048]{2,1,0:T(8,12...) custom-call(s32[10,128]{1,0:T(8,128)} %bitcast.2, ...), custom_call_target="tpu_custom_call" | custom-call | flops 60000002048 | bytes 60000000 | tf_op jit(solution)/shard_map/pallas_call | solution.py:586
  191.8 9.9 %shard_map.103 = (bf16[128,2048]{1,0:T(8,128)(2,1)}, bf16[2,2048,512]{2,1,0:T(8,128)(2,1)}, bf16[2,2048,512]{2,1,0:T(8,128)(2,1)}, bf16[2,512,2048]{2,1,0:T(8,128)(2,1)}) custom-call(bf16[128,2048]{1,0:T(8,128)(2,1)} %get-tuple-element.8.refs_0_, bf16[2,2048,512]{2,1,0:T(8,128)(2,1)} %get-tuple-element.9.refs_1_, ...), custom_call_target="tpu_custom_call" | custom-call | bytes 26000000 | tf_op jit(solution)/shard_map/pallas_call | solution.py:541

commit v2 on v1

--- a/solution.py
+++ b/solution.py
@@ -141,7 +141,7 @@
     def store_w(n, e):
         return pltpu.make_async_copy(wbuf[n], outs[n].at[e], o_sem.at[n])
 
-    step = (1, 2, 3)
+    step = (2, 1, 3)
 
     barrier = pltpu.get_barrier_semaphore()
     for axis in range(3):
@@ -521,10 +521,10 @@
 def copy_kernel(*refs):
     src, dst, held, sems = refs[:4], refs[4:8], refs[8:12], refs[12]
     moves = [(0, (pl.ds(0, TOK),))]
-    for k in range(8):
+    for k in range(4):
         for n in (1, 2, 3):
-            size = src[n].shape[1] // 4
-            moves.append((n, (k // 4, pl.ds((k % 4) * size, size))))
+            size = src[n].shape[1] // 2
+            moves.append((n, (k // 2, pl.ds((k % 2) * size, size))))
     into = [pltpu.make_async_copy(src[n].at[at], held[n].at[at], sems.at[0, j]) for j, (n, at) in enumerate(moves)]
     out = [pltpu.make_async_copy(held[n].at[at], dst[n].at[at], sems.at[1, j]) for j, (n, at) in enumerate(moves)]
     for one in into:

time: 202 us -> 202 us (level)
  no operation moved by 1% of the time
where the time goes in v2:
time: 202 us
  Pallas kernels  201 us (100%)
    pallas_call x1, Pallas kernels, per_device(): pl.pallas_call(kernel, out_shape=[jax.ShapeDtypeStruct(tokens.shape, BF),...  191 us
    pallas_call x1, Pallas kernels, hand_over(): pl.pallas_call(copy_kernel, out_shape=[jax.ShapeDtypeStruct(a.shape, a.dt...  9.81 us

profile of v2, /device:TPU:0, one launch (start us, length us, event | category | flops | bytes accessed | tf_op | source)
XLA Modules:
  0.0 201.6 jit_solution(14275754915139495747)
XLA Ops:
  0.6 191.0 %shard_map.102 = (bf16[128,2048]{1,0:T(8,128)(2,1)}, bf16[2,2048,512]{2,1,0:T(8,128)(2,1)}, bf16[2,2048,512]{2,1,0:T(8,128)(2,1)}, bf16[2,512,2048]{2,1,0:T(8,12...) custom-call(s32[10,128]{1,0:T(8,128)} %bitcast.2, ...), custom_call_target="tpu_custom_call" | custom-call | flops 60000002048 | bytes 60000000 | tf_op jit(solution)/shard_map/pallas_call | solution.py:586
  191.6 9.8 %shard_map.103 = (bf16[128,2048]{1,0:T(8,128)(2,1)}, bf16[2,2048,512]{2,1,0:T(8,128)(2,1)}, bf16[2,2048,512]{2,1,0:T(8,128)(2,1)}, bf16[2,512,2048]{2,1,0:T(8,128)(2,1)}) custom-call(bf16[128,2048]{1,0:T(8,128)(2,1)} %get-tuple-element.8.refs_0_, bf16[2,2048,512]{2,1,0:T(8,128)(2,1)} %get-tuple-element.9.refs_1_, ...), custom_call_target="tpu_custom_call" | custom-call | bytes 26000000 | tf_op jit(solution)/shard_map/pallas_call | solution.py:541
